TPU v7x, 32 devices: a whole 2x2x4 slice. The times are simulated.
32 devices in a mesh: row: 4 (over y, x), col: 8 (over z, core).
Axes of the slice: x: 2, y: 2, z: 4, core: 2. Of those that a mesh axis runs over, the one named last changes fastest.
Arguments:
- amplitudes: bfloat16 [32, 256, 32, 256], P('row', None, 'col'), may hold values from -6 to 6
- factors: bfloat16 [32, 256, 384], P('row'), may hold values from -0.109375 to 0.109375
- occ_energy: float32 [32], replicated, may hold values from -2 to -0.5
- vir_energy: float32 [256], replicated, may hold values from 0.2 to 3
Outputs:
- residual: float32 [32, 256, 32, 256], P('row', None, 'col')
All inputs are finite; a program needn't handle non-finite values.
Results may differ from a plain program's by a relative error of at most 0.0029.
Values may be sent and summed in bfloat16 or wider, within the bound.
A program may use at most 192 MiB of HBM per device.

v0:
```python
import jax
import jax.numpy as jnp
from jax import lax
from jax.sharding import PartitionSpec as P


def single_term(left_one, right_flat, right_turned, amplitude_rows):
    virtual = left_one.shape[0]
    coulomb = lax.dot_general(
        left_one, right_flat, (((1,), (1,)), ((), ())), preferred_element_type=jnp.float32
    )
    exchange_part = lax.dot_general(
        right_turned, left_one, (((1,), (1,)), ((), ())), preferred_element_type=jnp.float32
    )
    coupling = (2.0 * coulomb - exchange_part.reshape(virtual, -1)).astype(jnp.bfloat16)
    return jnp.dot(coupling, amplitude_rows, preferred_element_type=jnp.float32)


def prepare(right_factors, amplitude_block):
    right_count, virtual, auxiliary = right_factors.shape
    right_flat = right_factors.reshape(right_count * virtual, auxiliary)
    right_turned = right_factors.transpose(1, 0, 2).reshape(virtual * right_count, auxiliary)
    amplitude_rows = amplitude_block.reshape(right_count * virtual, -1)
    return (right_flat, right_turned, amplitude_rows)


def body(amplitudes, factors, occ_energy, vir_energy):
    own_rows = factors.shape[0]
    virtual = factors.shape[1]
    pairs_cols = amplitudes.shape[2]
    all_factors = lax.all_gather(factors, "row", axis=0, tiled=True)
    right_flat, right_turned, amplitude_rows = prepare(factors, amplitudes)

    def add_left(position, buffer):
        left_one = lax.dynamic_index_in_dim(all_factors, position, 0, keepdims=False)
        term = single_term(left_one, right_flat, right_turned, amplitude_rows)
        term = term.reshape(1, virtual, pairs_cols, virtual)
        return lax.dynamic_update_slice_in_dim(buffer, term, position, 0)

    buffer = jnp.zeros((lax.axis_size("row") * own_rows, virtual, pairs_cols, virtual), jnp.float32)
    summed = lax.psum_scatter(
        lax.fori_loop(0, lax.axis_size("row") * own_rows, add_left, buffer),
        "row",
        scatter_dimension=0,
        tiled=True,
    )
    swapped = summed.transpose(2, 3, 0, 1)
    section_one = lax.all_to_all(swapped, "row", split_axis=1, concat_axis=2, tiled=True)
    section_two = lax.all_to_all(section_one, "col", split_axis=2, concat_axis=0, tiled=True)
    mirrored = lax.all_to_all(section_two, "row", split_axis=0, concat_axis=1, tiled=True)
    row_place = lax.axis_index("row")
    col_place = lax.axis_index("col")
    occ_first = lax.dynamic_slice_in_dim(occ_energy, row_place * own_rows, own_rows, 0)
    occ_second = lax.dynamic_slice_in_dim(occ_energy, col_place * pairs_cols, pairs_cols, 0)
    denominator = (
        vir_energy[None, :, None, None]
        + vir_energy[None, None, None, :]
        - occ_first[:, None, None, None]
        - occ_second[None, None, :, None]
    )
    return (summed + mirrored) / denominator


def solution(mesh):
    in_specs = (P("row", None, "col", None), P("row", None, None), P(), P())
    out_specs = P("row", None, "col", None)
    return jax.shard_map(body, mesh=mesh, in_specs=in_specs, out_specs=out_specs, check_vma=False)
```

profile of v0, /device:TPU:18, one launch (start us, length us, event | category | flops | bytes accessed | tf_op | source)
XLA Modules:
  0.0 1244.7 jit_solution(10560490850054601343)
XLA Ops:
  10.8 5.2 copy.45
  16.0 64.4 %all-gather.2.cloned.1.call-done = bf16[32,256,384]{2,1,0:T(8,128)(2,1)} async-done(((bf16[8,256,384]{2,1,0:T(8,128)(2,1)}), bf16[32,256,384]{2,1,0:T(8,128)(2,1)}) %all-gather.2.cloned.1.call-update) | async-done | bytes 6291472 | tf_op jit(solution)/shard_map/all_gather | solution.py:31
  80.4 444.5 %while.13 = (s32[]{:T(128)}, f32[32,256,4,256]{3,1,2,0:T(8,128)}, bf16[32,256,384]{2,1,0:T(8,128)(2,1)}, bf16[2048,384]{1,0:T(8,128)(2,1)}, bf16[2048,384]{1,0:T...) while((s32[]{:T(128)}, f32[32,256,4,256]{3,1,2,0:T(8,128)}, bf16[32,256,384]{2,1,0:T(8,128)(2,1)}, ...), condition=%wide.region_1.2_spmd, body=%wide.region_0.1_spmd.sunk | while | flops 1880621056 | bytes 25559136 | solution.py:42
  87.4 5.2 fusion.28
  101.3 5.2 fusion.28
  143.0 5.2 fusion.28
  170.7 5.2 fusion.28
  184.6 5.2 fusion.28
  226.3 5.2 fusion.28
  240.2 5.2 fusion.28
  254.1 5.2 fusion.28
  268.0 5.2 fusion.28
  295.8 5.2 fusion.28
  351.3 5.2 fusion.28
  420.8 5.2 fusion.28
  462.5 5.2 fusion.28
  524.9 288.7 %reduce-scatter.2.cloned.1.call-done = f32[8,256,4,256]{3,1,2,0:T(8,128)} async-done(((f32[32,256,4,256]{3,1,2,0:T(8,128)}), f32[8,256,4,256]{3,1,2,0:T(8,128)}) %reduce-scatter.2.cloned.1.call-update) | async-done | bytes 8388624 | tf_op jit(solution)/shard_map/reduce_scatter | solution.py:41
  813.6 10.4 copy.33
  824.0 96.7 %all_to_all.54 = f32[4,256,8,256]{3,2,0,1:T(8,128)S(1)} all-to-all(f32[4,256,8,256]{3,2,0,1:T(8,128)} %copy.33), channel_id=1, replica_groups=mesh['row'=4,'col'=8] {'row'}, dimensions={1} | all-to-all | bytes 16777216 | tf_op jit(solution)/shard_map/all_to_all | solution.py:48
  926.9 185.7 %all_to_all.55 = f32[4,64,32,256]{3,1,0,2:T(8,128)S(1)} all-to-all(f32[4,64,32,256]{3,1,0,2:T(8,128)S(1)} %copy.36), channel_id=1, replica_groups=mesh['row'=4,'col'=8] {'col'}, dimensions={2} | all-to-all | bytes 16777216 | tf_op jit(solution)/shard_map/all_to_all | solution.py:49
  1116.6 6.8 all-to-all-start.2
  1123.9 91.4 %all-to-all-done.2 = f32[32,64,4,256]{3,1,2,0:T(8,128)} async-done(((f32[32,64,4,256]{3,1,2,0:T(8,128)}), f32[32,64,4,256]{3,1,2,0:T(8,128)}, u32[]{:S(2)}, u32[]{:S(2)}) %all-to-all-start.2) | async-done | bytes 8388640 | tf_op jit(solution)/shard_map/all_to_all | solution.py:50
  1219.3 6.4 fusion.13
  1225.7 12.2 copy.40
  (197 shorter events, 395.1 us)
Async XLA Ops:
  6.5 73.9 %all-gather.2.cloned.1.call-start = ((), (), s32[]{:S(2)}) async-start(), calls=%async_computation.4 | async-start | bytes 7864320 | tf_op jit(solution)/shard_map/all_gather | solution.py:31
  7.3 806.4 %reduce-scatter.2.cloned.1.call-start = ((), (), s32[]{:S(2)}) async-start(), calls=%async_computation.5 | async-start | bytes 41943040 | tf_op jit(solution)/shard_map/reduce_scatter | solution.py:41
  1116.6 6.9 copy-start.1
  1116.6 7.0 copy-start
  1116.6 98.7 %all-to-all-start.2 = ((f32[32,64,4,256]{3,1,2,0:T(8,128)}), f32[32,64,4,256]{3,1,2,0:T(8,128)}, u32[]{:S(2)}, u32[]{:S(2)}) async-start(f32[32,64,4,256]{3,1,2,0:T(8,128)} %bitcast.50), calls=%async_computation.3 | async-start | bytes 16777216 | tf_op jit(solution)/shard_map/all_to_all | solution.py:50
Sparse Core Ops, SparseCore 0:
  9.2 71.1 all-gather.1
  525.0 288.5 reduce-scatter.1
where the time goes:
time: 1250 us; the launch traced here: 1240 us
  waiting for transfers between devices  445 us (36%)
  blocking collectives  282 us (23%)
  matrix products  281 us (22%)
  local copies, waits for them, and re-layouts  209 us (17%)
  between operations  13.5 us (1%)
    reduce_scatter x1, waiting for transfers between devices, body(): lax.psum_scatter(lax.fori_loop(0, lax.axis_size('row') * own_rows, add_le...  289 us
    all_to_all x1, blocking collectives, body(): lax.all_to_all(section_one, 'col', split_axis=2, concat_axis=0, tiled=True)  186 us
    dot_general x32, matrix products, single_term(): return jnp.dot(coupling, amplitude_rows, preferred_element_type=jnp.float32)  166 us
    dot_general x32, matrix products, single_term(): lax.dot_general(right_turned, left_one, (((1,), (1,)), ((), ())), preferr...  115 us
    all_to_all x1, blocking collectives, body(): lax.all_to_all(swapped, 'row', split_axis=1, concat_axis=2, tiled=True)  96.7 us
    all_to_all x1, waiting for transfers between devices, body(): lax.all_to_all(section_two, 'row', split_axis=0, concat_axis=1, tiled=True)  91.4 us
    all_gather x1, waiting for transfers between devices, body(): all_factors = lax.all_gather(factors, 'row', axis=0, tiled=True)  64.4 us
    dot_general x32, local copies, waits for them, and re-layouts, single_term(): lax.dot_general(right_turned, left_one, (((1,), (1,)), ((), ())), preferr...  61.4 us
  transfers between devices with their start and end apart: 3, of which 3 were waited for; matrix products, arithmetic and copies ran while one was open for 1% of the time, Pallas kernels for 0%

commit v1 on v0

v1 whole, which is shorter than its diff:
```python
import jax
import jax.numpy as jnp
from jax import lax
from jax.sharding import PartitionSpec as P

BF16 = jnp.bfloat16
F32 = jnp.float32


def denominators(occ_energy, vir_energy, rows, cols):
    row_place = lax.axis_index("row")
    col_place = lax.axis_index("col")
    occ_first = lax.dynamic_slice_in_dim(occ_energy, row_place * rows, rows, 0)
    occ_second = lax.dynamic_slice_in_dim(occ_energy, col_place * cols, cols, 0)
    return (
        vir_energy[None, :, None, None]
        + vir_energy[None, None, None, :]
        - occ_first[:, None, None, None]
        - occ_second[None, None, :, None]
    )


def coupling_of(left_one, right):
    count, virtual, _ = right.shape
    coulomb = lax.dot_general(
        left_one, right.reshape(count * virtual, -1), (((1,), (1,)), ((), ())), preferred_element_type=F32
    )
    exchange = lax.dot_general(right, left_one, (((2,), (1,)), ((), ())), preferred_element_type=F32)
    exchange = exchange.transpose(1, 0, 2).reshape(virtual, count * virtual)
    return (2.0 * coulomb - exchange).astype(BF16)


def general_body(amplitudes, factors, occ_energy, vir_energy):
    rows, virtual, cols, _ = amplitudes.shape
    all_factors = lax.all_gather(factors, "row", axis=0, tiled=True)
    all_amplitudes = lax.all_gather(amplitudes, "row", axis=0, tiled=True)
    columns = all_amplitudes.reshape(-1, cols * virtual)

    def one(left_one):
        return jnp.dot(coupling_of(left_one, all_factors), columns, preferred_element_type=F32)

    summed = lax.map(one, factors).reshape(rows, virtual, cols, virtual)
    swapped = summed.astype(BF16).transpose(2, 3, 0, 1)
    section_one = lax.all_to_all(swapped, "row", split_axis=1, concat_axis=2, tiled=True)
    section_two = lax.all_to_all(section_one, "col", split_axis=2, concat_axis=0, tiled=True)
    mirrored = lax.all_to_all(section_two, "row", split_axis=0, concat_axis=1, tiled=True)
    return (summed + mirrored) / denominators(occ_energy, vir_energy, rows, cols)


def paired_body(amplitudes, factors, occ_energy, vir_energy):
    rows, virtual, cols, _ = amplitudes.shape
    ranks = lax.axis_size("row")
    side = lax.rem(lax.axis_index("col"), 2)
    swap = [(s, s ^ 1) for s in range(2 * ranks)]
    half = rows // 2
    per = cols // ranks
    all_factors = lax.all_gather(factors, "row", axis=0, tiled=True)
    own = lax.all_to_all(amplitudes, "row", split_axis=2, concat_axis=0, tiled=True)
    own = own.reshape(-1, per * virtual)
    other = lax.ppermute(own, "col", swap)
    columns = jnp.concatenate([own, other], axis=1)
    split = all_factors.reshape(ranks, 2, half, virtual, -1)
    left = lax.dynamic_index_in_dim(split, side, 1, keepdims=False).reshape(ranks * half, virtual, -1)

    def one(left_one):
        product = jnp.dot(coupling_of(left_one, all_factors), columns, preferred_element_type=F32)
        return product.astype(BF16)

    sums = lax.map(one, left).reshape(ranks, half, virtual, 2, per, virtual)
    sums = sums.transpose(3, 0, 1, 4, 2, 5)
    direct = jnp.stack([sums[0], lax.ppermute(sums[1], "col", swap)], axis=1)
    direct = lax.all_to_all(direct, "row", split_axis=0, concat_axis=0, tiled=True)
    groups = [[2 * z + c for z in range(ranks)] for c in range(2)]
    mirror = lax.all_to_all(sums.swapaxes(0, 1), "col", split_axis=0, concat_axis=0, axis_index_groups=groups, tiled=True)
    mirror = lax.all_to_all(mirror, "row", split_axis=0, concat_axis=0, tiled=True)
    direct = direct.transpose(1, 2, 4, 0, 3, 5).reshape(2, half, virtual, cols, virtual)
    mirror = mirror.transpose(1, 0, 3, 5, 2, 4).reshape(2, half, virtual, cols, virtual)
    total = direct.astype(F32) + mirror.astype(F32)
    total = jnp.where(side == 0, total, total[::-1]).reshape(rows, virtual, cols, virtual)
    return total / denominators(occ_energy, vir_energy, rows, cols)


def solution(mesh):
    ranks, places = mesh.shape["row"], mesh.shape["col"]

    def body(amplitudes, factors, occ_energy, vir_energy):
        rows, _, cols, _ = amplitudes.shape
        paired = places == 2 * ranks and rows == 2 * cols and cols == ranks
        chosen = paired_body if paired else general_body
        return chosen(amplitudes, factors, occ_energy, vir_energy)

    in_specs = (P("row", None, "col", None), P("row", None, None), P(), P())
    out_specs = P("row", None, "col", None)
    return jax.shard_map(body, mesh=mesh, in_specs=in_specs, out_specs=out_specs, check_vma=False)
```

time: 1250 us -> 850 us (0.68)
  waiting for transfers between devices: 445 us -> 120 us
  blocking collectives: 282 us -> 164 us
  matrix products: 281 us -> 331 us
  local copies, waits for them, and re-layouts: 209 us -> 181 us
  other arithmetic: 6.73 us -> 22.8 us
    reduce_scatter x1 -> x0, waiting for transfers between devices: 289 us -> none  [body(): lax.psum_scatter(lax.fori_loop(0, lax.axis_size('row') * own_rows, add_le...]
    all_to_all x2, blocking collectives: 282 us -> 164 us  [the longest x1 96.4 us: paired_body(): lax.all_to_all(sums.swapaxes(0, 1), 'col', split_axis=0, concat_axis=0, a...]
    reshape x64 -> x16, local copies, waits for them, and re-layouts: 63.6 us -> 143 us  [coupling_of(): exchange = exchange.transpose(1, 0, 2).reshape(virtual, count * virtual)]
    dot_general x32 -> x0, local copies, waits for them, and re-layouts: 61.4 us -> none  [single_term(): lax.dot_general(right_turned, left_one, (((1,), (1,)), ((), ())), preferr...]
    dot_general x64 -> x32, matrix products: 281 us -> 331 us  [the longest x16 195 us: one(): jnp.dot(coupling_of(left_one, all_factors), columns, preferred_element_ty...]
    all_gather x1, waiting for transfers between devices: 64.4 us -> 21.6 us  [paired_body(): all_factors = lax.all_gather(factors, 'row', axis=0, tiled=True)]
    dynamic_update_slice x32, local copies, waits for them, and re-layouts: 38.1 us -> 13.9 us  [paired_body(): sums = lax.map(one, left).reshape(ranks, half, virtual, 2, per, virtual)]
    another operation x0 -> x3, local copies, waits for them, and re-layouts: none -> 17.3 us  [the longest x2 9.85 us: paired_body(): direct = jnp.stack([sums[0], lax.ppermute(sums[1], 'col', swap)], axis=1)]
  transfers between devices with their start and end apart: 3 -> 5, of which waited for: 3 -> 5; matrix products, arithmetic and copies ran while one was open for 1% -> 2% of each run, Pallas kernels for 0% -> 0%
where the time goes in v1:
time: 850 us; the launch traced here: 843 us
  matrix products  331 us (39%)
  local copies, waits for them, and re-layouts  181 us (21%)
  blocking collectives  164 us (19%)
  waiting for transfers between devices  120 us (14%)
  other arithmetic  22.8 us (3%)
  between operations  13.5 us (2%)
  starting transfers between devices  11 us (1%)
    dot_general x16, matrix products, one(): jnp.dot(coupling_of(left_one, all_factors), columns, preferred_element_ty...  195 us
    reshape x16, local copies, waits for them, and re-layouts, coupling_of(): exchange = exchange.transpose(1, 0, 2).reshape(virtual, count * virtual)  143 us
    dot_general x16, matrix products, coupling_of(): lax.dot_general(right, left_one, (((2,), (1,)), ((), ())), preferred_elem...  136 us
    all_to_all x1, blocking collectives, paired_body(): lax.all_to_all(sums.swapaxes(0, 1), 'col', split_axis=0, concat_axis=0, a...  96.4 us
    all_to_all x1, blocking collectives, paired_body(): lax.all_to_all(amplitudes, 'row', split_axis=2, concat_axis=0, tiled=True)  67.8 us
    all_to_all x1, waiting for transfers between devices, paired_body(): lax.all_to_all(mirror, 'row', split_axis=0, concat_axis=0, tiled=True)  45.8 us
    all_to_all x1, waiting for transfers between devices, paired_body(): lax.all_to_all(direct, 'row', split_axis=0, concat_axis=0, tiled=True)  40 us
    all_gather x1, waiting for transfers between devices, paired_body(): all_factors = lax.all_gather(factors, 'row', axis=0, tiled=True)  21.6 us
  transfers between devices with their start and end apart: 5, of which 5 were waited for; matrix products, arithmetic and copies ran while one was open for 2% of the time, Pallas kernels for 0%

profile of v1, /device:TPU:18, one launch (start us, length us, event | category | flops | bytes accessed | tf_op | source)
XLA Modules:
  0.0 842.9 jit_solution(15154243842733750737)
XLA Ops:
  10.2 67.8 %all_to_all.30 = bf16[8,256,4,256]{3,1,0,2:T(8,128)(2,1)} all-to-all(bf16[8,256,4,256]{3,1,0,2:T(8,128)(2,1)S(1)} %copy.15), channel_id=1, replica_groups=mesh['row'=4,'col'=8] {'row'}, dimensions={2} | all-to-all | bytes 8388608 | tf_op jit(solution)/shard_map/all_to_all | solution.py:58
  93.0 21.6 %all-gather.2.cloned.1.call-done = bf16[32,256,384]{2,1,0:T(8,128)(2,1)} async-done(((bf16[8,256,384]{2,1,0:T(8,128)(2,1)}), bf16[32,256,384]{2,1,0:T(8,128)(2,1)}) %all-gather.2.cloned.1.call-update) | async-done | bytes 6291472 | tf_op jit(solution)/shard_map/all_gather | solution.py:57
  118.7 487.3 %while.10 = (s32[]{:T(128)}, bf16[16,256,512]{1,2,0:T(8,128)(2,1)}, bf16[16,256,384]{2,1,0:T(8,128)(2,1)}, bf16[32,256,384]{2,1,0:T(8,128)(2,1)}, bf16[8192,512]{1,0:T(8,128)(2,1)}, /*index=5*/s32[]{:T(128)}) while((s32[]{:T(128)}, bf16[16,256,512]{1,2,0:T(8,128)(2,1)}, bf16[16,256,384]{2,1,0:T(8,128)(2,1)}, bf16[32,256,384]{2,1,0:T(8,128)(2,1)}, ...), condition=%wide.region_1.2_spmd, body=%wide.region_0.1_spmd.sunk | while | flops 5375131648 | bytes 56231492 | solution.py:69
  136.1 12.2 %fusion.30 = bf16[1,256,512]{2,1,0:T(8,128)(2,1)S(1)} fusion(bf16[8192,512]{1,0:T(8,128)(2,1)} %get-tuple-element.92, f32[256,8192]{1,0:T(8,128)} %copy.30, bf16[8192,384]{1,0:T(8,128)(2,1)} %bitcast.62, bf16[16,256,384]{2,1,0:T(8,128)(2,1)} %get-tuple-element.90, s32[]{:T(128)} %get-tuple-element.82), kind=kOutput, calls=%fused_computation.4.clone.1 | convolution fusion | flops 3764518912 | bytes 23527936 | tf_op jit(solution)/shard_map/while/body/eval_jaxpr/dot_general | solution.py:66
  157.6 8.9 %copy.30 = f32[256,8192]{1,0:T(8,128)} copy(f32[256,8192]{0,1:T(8,128)} %bitcast.60) | data formatting | bytes 16777216 | tf_op jit(solution)/shard_map/while/body/eval_jaxpr/reshape | solution.py:29
  166.5 12.2 %fusion.30 = bf16[1,256,512]{2,1,0:T(8,128)(2,1)S(1)} fusion(bf16[8192,512]{1,0:T(8,128)(2,1)} %get-tuple-element.92, f32[256,8192]{1,0:T(8,128)} %copy.30, bf16[8192,384]{1,0:T(8,128)(2,1)} %bitcast.62, bf16[16,256,384]{2,1,0:T(8,128)(2,1)} %get-tuple-element.90, s32[]{:T(128)} %get-tuple-element.82), kind=kOutput, calls=%fused_computation.4.clone.1 | convolution fusion | flops 3764518912 | bytes 23527936 | tf_op jit(solution)/shard_map/while/body/eval_jaxpr/dot_general | solution.py:66
  196.9 12.2 %fusion.30 = bf16[1,256,512]{2,1,0:T(8,128)(2,1)S(1)} fusion(bf16[8192,512]{1,0:T(8,128)(2,1)} %get-tuple-element.92, f32[256,8192]{1,0:T(8,128)} %copy.30, bf16[8192,384]{1,0:T(8,128)(2,1)} %bitcast.62, bf16[16,256,384]{2,1,0:T(8,128)(2,1)} %get-tuple-element.90, s32[]{:T(128)} %get-tuple-element.82), kind=kOutput, calls=%fused_computation.4.clone.1 | convolution fusion | flops 3764518912 | bytes 23527936 | tf_op jit(solution)/shard_map/while/body/eval_jaxpr/dot_general | solution.py:66
  218.5 8.9 %copy.30 = f32[256,8192]{1,0:T(8,128)} copy(f32[256,8192]{0,1:T(8,128)} %bitcast.60) | data formatting | bytes 16777216 | tf_op jit(solution)/shard_map/while/body/eval_jaxpr/reshape | solution.py:29
  227.4 12.2 %fusion.30 = bf16[1,256,512]{2,1,0:T(8,128)(2,1)S(1)} fusion(bf16[8192,512]{1,0:T(8,128)(2,1)} %get-tuple-element.92, f32[256,8192]{1,0:T(8,128)} %copy.30, bf16[8192,384]{1,0:T(8,128)(2,1)} %bitcast.62, bf16[16,256,384]{2,1,0:T(8,128)(2,1)} %get-tuple-element.90, s32[]{:T(128)} %get-tuple-element.82), kind=kOutput, calls=%fused_computation.4.clone.1 | convolution fusion | flops 3764518912 | bytes 23527936 | tf_op jit(solution)/shard_map/while/body/eval_jaxpr/dot_general | solution.py:66
  257.9 12.2 %fusion.30 = bf16[1,256,512]{2,1,0:T(8,128)(2,1)S(1)} fusion(bf16[8192,512]{1,0:T(8,128)(2,1)} %get-tuple-element.92, f32[256,8192]{1,0:T(8,128)} %copy.30, bf16[8192,384]{1,0:T(8,128)(2,1)} %bitcast.62, bf16[16,256,384]{2,1,0:T(8,128)(2,1)} %get-tuple-element.90, s32[]{:T(128)} %get-tuple-element.82), kind=kOutput, calls=%fused_computation.4.clone.1 | convolution fusion | flops 3764518912 | bytes 23527936 | tf_op jit(solution)/shard_map/while/body/eval_jaxpr/dot_general | solution.py:66
  288.3 12.2 %fusion.30 = bf16[1,256,512]{2,1,0:T(8,128)(2,1)S(1)} fusion(bf16[8192,512]{1,0:T(8,128)(2,1)} %get-tuple-element.92, f32[256,8192]{1,0:T(8,128)} %copy.30, bf16[8192,384]{1,0:T(8,128)(2,1)} %bitcast.62, bf16[16,256,384]{2,1,0:T(8,128)(2,1)} %get-tuple-element.90, s32[]{:T(128)} %get-tuple-element.82), kind=kOutput, calls=%fused_computation.4.clone.1 | convolution fusion | flops 3764518912 | bytes 23527936 | tf_op jit(solution)/shard_map/while/body/eval_jaxpr/dot_general | solution.py:66
  318.7 12.2 %fusion.30 = bf16[1,256,512]{2,1,0:T(8,128)(2,1)S(1)} fusion(bf16[8192,512]{1,0:T(8,128)(2,1)} %get-tuple-element.92, f32[256,8192]{1,0:T(8,128)} %copy.30, bf16[8192,384]{1,0:T(8,128)(2,1)} %bitcast.62, bf16[16,256,384]{2,1,0:T(8,128)(2,1)} %get-tuple-element.90, s32[]{:T(128)} %get-tuple-element.82), kind=kOutput, calls=%fused_computation.4.clone.1 | convolution fusion | flops 3764518912 | bytes 23527936 | tf_op jit(solution)/shard_map/while/body/eval_jaxpr/dot_general | solution.py:66
  349.2 12.2 %fusion.30 = bf16[1,256,512]{2,1,0:T(8,128)(2,1)S(1)} fusion(bf16[8192,512]{1,0:T(8,128)(2,1)} %get-tuple-element.92, f32[256,8192]{1,0:T(8,128)} %copy.30, bf16[8192,384]{1,0:T(8,128)(2,1)} %bitcast.62, bf16[16,256,384]{2,1,0:T(8,128)(2,1)} %get-tuple-element.90, s32[]{:T(128)} %get-tuple-element.82), kind=kOutput, calls=%fused_computation.4.clone.1 | convolution fusion | flops 3764518912 | bytes 23527936 | tf_op jit(solution)/shard_map/while/body/eval_jaxpr/dot_general | solution.py:66
  379.7 12.2 %fusion.30 = bf16[1,256,512]{2,1,0:T(8,128)(2,1)S(1)} fusion(bf16[8192,512]{1,0:T(8,128)(2,1)} %get-tuple-element.92, f32[256,8192]{1,0:T(8,128)} %copy.30, bf16[8192,384]{1,0:T(8,128)(2,1)} %bitcast.62, bf16[16,256,384]{2,1,0:T(8,128)(2,1)} %get-tuple-element.90, s32[]{:T(128)} %get-tuple-element.82), kind=kOutput, calls=%fused_computation.4.clone.1 | convolution fusion | flops 3764518912 | bytes 23527936 | tf_op jit(solution)/shard_map/while/body/eval_jaxpr/dot_general | solution.py:66
  410.1 12.2 %fusion.30 = bf16[1,256,512]{2,1,0:T(8,128)(2,1)S(1)} fusion(bf16[8192,512]{1,0:T(8,128)(2,1)} %get-tuple-element.92, f32[256,8192]{1,0:T(8,128)} %copy.30, bf16[8192,384]{1,0:T(8,128)(2,1)} %bitcast.62, bf16[16,256,384]{2,1,0:T(8,128)(2,1)} %get-tuple-element.90, s32[]{:T(128)} %get-tuple-element.82), kind=kOutput, calls=%fused_computation.4.clone.1 | convolution fusion | flops 3764518912 | bytes 23527936 | tf_op jit(solution)/shard_map/while/body/eval_jaxpr/dot_general | solution.py:66
  440.6 12.2 %fusion.30 = bf16[1,256,512]{2,1,0:T(8,128)(2,1)S(1)} fusion(bf16[8192,512]{1,0:T(8,128)(2,1)} %get-tuple-element.92, f32[256,8192]{1,0:T(8,128)} %copy.30, bf16[8192,384]{1,0:T(8,128)(2,1)} %bitcast.62, bf16[16,256,384]{2,1,0:T(8,128)(2,1)} %get-tuple-element.90, s32[]{:T(128)} %get-tuple-element.82), kind=kOutput, calls=%fused_computation.4.clone.1 | convolution fusion | flops 3764518912 | bytes 23527936 | tf_op jit(solution)/shard_map/while/body/eval_jaxpr/dot_general | solution.py:66
  471.1 12.2 %fusion.30 = bf16[1,256,512]{2,1,0:T(8,128)(2,1)S(1)} fusion(bf16[8192,512]{1,0:T(8,128)(2,1)} %get-tuple-element.92, f32[256,8192]{1,0:T(8,128)} %copy.30, bf16[8192,384]{1,0:T(8,128)(2,1)} %bitcast.62, bf16[16,256,384]{2,1,0:T(8,128)(2,1)} %get-tuple-element.90, s32[]{:T(128)} %get-tuple-element.82), kind=kOutput, calls=%fused_computation.4.clone.1 | convolution fusion | flops 3764518912 | bytes 23527936 | tf_op jit(solution)/shard_map/while/body/eval_jaxpr/dot_general | solution.py:66
  501.5 12.2 %fusion.30 = bf16[1,256,512]{2,1,0:T(8,128)(2,1)S(1)} fusion(bf16[8192,512]{1,0:T(8,128)(2,1)} %get-tuple-element.92, f32[256,8192]{1,0:T(8,128)} %copy.30, bf16[8192,384]{1,0:T(8,128)(2,1)} %bitcast.62, bf16[16,256,384]{2,1,0:T(8,128)(2,1)} %get-tuple-element.90, s32[]{:T(128)} %get-tuple-element.82), kind=kOutput, calls=%fused_computation.4.clone.1 | convolution fusion | flops 3764518912 | bytes 23527936 | tf_op jit(solution)/shard_map/while/body/eval_jaxpr/dot_general | solution.py:66
  532.0 12.2 %fusion.30 = bf16[1,256,512]{2,1,0:T(8,128)(2,1)S(1)} fusion(bf16[8192,512]{1,0:T(8,128)(2,1)} %get-tuple-element.92, f32[256,8192]{1,0:T(8,128)} %copy.30, bf16[8192,384]{1,0:T(8,128)(2,1)} %bitcast.62, bf16[16,256,384]{2,1,0:T(8,128)(2,1)} %get-tuple-element.90, s32[]{:T(128)} %get-tuple-element.82), kind=kOutput, calls=%fused_computation.4.clone.1 | convolution fusion | flops 3764518912 | bytes 23527936 | tf_op jit(solution)/shard_map/while/body/eval_jaxpr/dot_general | solution.py:66
  562.5 12.2 %fusion.30 = bf16[1,256,512]{2,1,0:T(8,128)(2,1)S(1)} fusion(bf16[8192,512]{1,0:T(8,128)(2,1)} %get-tuple-element.92, f32[256,8192]{1,0:T(8,128)} %copy.30, bf16[8192,384]{1,0:T(8,128)(2,1)} %bitcast.62, bf16[16,256,384]{2,1,0:T(8,128)(2,1)} %get-tuple-element.90, s32[]{:T(128)} %get-tuple-element.82), kind=kOutput, calls=%fused_computation.4.clone.1 | convolution fusion | flops 3764518912 | bytes 23527936 | tf_op jit(solution)/shard_map/while/body/eval_jaxpr/dot_general | solution.py:66
  592.9 12.2 %fusion.30 = bf16[1,256,512]{2,1,0:T(8,128)(2,1)S(1)} fusion(bf16[8192,512]{1,0:T(8,128)(2,1)} %get-tuple-element.92, f32[256,8192]{1,0:T(8,128)} %copy.30, bf16[8192,384]{1,0:T(8,128)(2,1)} %bitcast.62, bf16[16,256,384]{2,1,0:T(8,128)(2,1)} %get-tuple-element.90, s32[]{:T(128)} %get-tuple-element.82), kind=kOutput, calls=%fused_computation.4.clone.1 | convolution fusion | flops 3764518912 | bytes 23527936 | tf_op jit(solution)/shard_map/while/body/eval_jaxpr/dot_general | solution.py:66
  635.2 40.0 %all-to-all-done.1 = bf16[4,2,4,1,256,256]{5,4,2,1,3,0:T(8,128)(2,1)} async-done(((bf16[4,2,4,1,256,256]{5,4,2,1,3,0:T(8,128)(2,1)}), bf16[4,2,4,1,256,256]{5,4,2,1,3,0:T(8,128)(2,1)}, u32[]{:S(2)}, u32[]{:S(2)}) %all-to-all-start.1) | async-done | bytes 4194336 | tf_op jit(solution)/shard_map/all_to_all | solution.py:72
  675.2 96.4 %all_to_all.31 = bf16[4,2,4,1,256,256]{4,2,5,1,3,0:T(4,128)(2,1)} all-to-all(bf16[4,2,4,1,256,256]{4,2,5,1,3,0:T(4,128)(2,1)} %copy.19), channel_id=1, replica_groups={{0,2,4,6},{1,3,5,7},{8,10,12,14},{9,11,13,15},{16,18,20,22},{17,19,21,2..., dimensions={0} | all-to-all | bytes 8388608 | tf_op jit(solution)/shard_map/all_to_all | solution.py:74
  777.6 45.8 %all-to-all-done.3 = bf16[4,2,4,1,256,256]{4,2,5,1,3,0:T(4,128)(2,1)} async-done(((bf16[4,2,4,1,256,256]{4,2,5,1,3,0:T(4,128)(2,1)}), bf16[4,2,4,1,256,256]{4,2,5,1,3,0:T(4,128)(2,1)}, u32[]{:S(2)}, u32[]{:S(2)}) %all-to-all-start.3) | async-done | bytes 4194336 | tf_op jit(solution)/shard_map/all_to_all | solution.py:75
  (89 shorter events, 345.0 us)
Async XLA Ops:
  6.5 108.0 %all-gather.2.cloned.1.call-start = ((), (), s32[]{:S(2)}) async-start(), calls=%async_computation.4 | async-start | bytes 7864320 | tf_op jit(solution)/shard_map/all_gather | solution.py:57
  78.0 7.5 collective-permute-start
  608.5 4.2 collective-permute-start.1
  622.4 52.8 %all-to-all-start.1 = ((bf16[4,2,4,1,256,256]{5,4,2,1,3,0:T(8,128)(2,1)}), bf16[4,2,4,1,256,256]{5,4,2,1,3,0:T(8,128)(2,1)}, u32[]{:S(2)}, u32[]{:S(2)}) async-start(bf16[4,2,4,1,256,256]{5,4,2,1,3,0:T(8,128)(2,1)} %copy.18), calls=%async_computation.1 | async-start | bytes 8388608 | tf_op jit(solution)/shard_map/all_to_all | solution.py:72
  771.6 5.5 copy-start.1
  771.6 5.7 copy-start
  771.6 51.8 %all-to-all-start.3 = ((bf16[4,2,4,1,256,256]{4,2,5,1,3,0:T(4,128)(2,1)}), bf16[4,2,4,1,256,256]{4,2,5,1,3,0:T(4,128)(2,1)}, u32[]{:S(2)}, u32[]{:S(2)}) async-start(bf16[4,2,4,1,256,256]{4,2,5,1,3,0:T(4,128)(2,1)} %all_to_all.31), calls=%async_computation.3 | async-start | bytes 8388608 | tf_op jit(solution)/shard_map/all_to_all | solution.py:75
Sparse Core Ops, SparseCore 0:
  9.2 105.3 all-gather.1
